TPU v7x, 1024 devices: a whole 4x8x16 slice. The times are simulated.
1024 devices in a mesh: wide: 64 (over z, x_lo, core), narrow: 16 (over x_hi, y).
Axes of the slice: x: 4 (x_hi: 2, x_lo: 2; x = x_hi * 2 + x_lo), y: 8, z: 16, core: 2. Of those that a mesh axis runs over, the one named last changes fastest.
Arguments:
- image_emb: bfloat16 [131072, 1152], P(('wide', 'narrow')), may hold values from -0.1875 to 0.1875
- text_feat: bfloat16 [131072, 1152], P(('wide', 'narrow')), may hold values from -0.75 to 0.75
- text_head: bfloat16 [1152, 1152], replicated, may hold values from -0.1875 to 0.1875
- row_counts: int32 [1024], P(('wide', 'narrow')), may hold values from 1 to 128, 81920 in all
- positive: int32 [131072], P(('wide', 'narrow')), may hold values from 0 to 127
- log_scale: float32 [1], replicated, may hold values from 2.5 to 4
- logit_bias: float32 [1], replicated, may hold values from -3 to -1
Outputs:
- image_grad: bfloat16 [131072, 1152], P(('wide', 'narrow'))
- text_grad: bfloat16 [131072, 1152], P(('wide', 'narrow'))
- head_grad: float32 [1152, 1152], P('narrow', 'wide')
- loss: float32 [1], replicated
Inputs may be any that keep to these rules, and one draw needn't show every extreme that they name: `row_counts`: live image rows of each block come first; some device has all 128 live.
All inputs are finite; a program needn't handle non-finite values.
Results may differ from a plain program's by a relative error of at most 0.0072.
Values may be sent and summed in bfloat16 or wider, within the bound.
A program may use at most 32 MiB of HBM per device.

v0:
```python
import jax
import jax.numpy as jnp
from jax import lax
from jax.sharding import PartitionSpec as P

EPSILON = 1e-06


def partner(value, axis, stride):
    return lax.ppermute(value, axis, [(i, i ^ 1 << stride) for i in range(lax.axis_size(axis))])


def unit_rows(values):
    row_norms = jnp.sqrt(jnp.sum(values * values, axis=-1, keepdims=True) + EPSILON)
    return (values / row_norms, row_norms)


def across_rows(left, right):
    return lax.dot_general(
        left, right, (((0,), (0,)), ((), ())), preferred_element_type=jnp.float32
    )


def per_device(image_emb, text_feat, text_head, row_counts, positive, log_scale, logit_bias):
    block_rows = image_emb.shape[0]
    device_total = lax.axis_size(("wide", "narrow"))
    near_bit = lax.axis_size("narrow").bit_length() - 2
    far_bit = device_total.bit_length() - 2
    logit_scale = jnp.exp(log_scale[0])
    offset_value = logit_bias[0]
    image_unit, image_norm = unit_rows(image_emb.astype(jnp.float32))
    image_bf = image_unit.astype(jnp.bfloat16)
    projected = jnp.dot(text_feat, text_head, preferred_element_type=jnp.float32)
    text_unit, text_norm = unit_rows(projected)
    text_bf = text_unit.astype(jnp.bfloat16)
    row_ids = jnp.arange(block_rows, dtype=jnp.int32)
    valid_rows = (row_ids < row_counts[0]).astype(jnp.float32)[:, None]
    own_sign = jnp.where(row_ids[None, :] == positive[:, None], 1.0, -1.0).astype(jnp.float32)
    weight_scale = logit_scale / block_rows

    def send_text(block, which_bit):
        return partner(block, ("wide", "narrow"), which_bit)

    near_text = send_text(text_bf, near_bit)
    far_text = send_text(text_bf, far_bit)
    diag_text = send_text(near_text, far_bit)

    def score_tile(partner_block, label_sign):
        products = lax.dot_general(
            image_bf, partner_block, (((1,), (1,)), ((), ())), preferred_element_type=jnp.float32
        )
        logits = logit_scale * products + offset_value
        losses = jnp.sum(jax.nn.softplus(-label_sign * logits) * valid_rows)
        weights = (
            -label_sign * jax.nn.sigmoid(-label_sign * logits) * valid_rows * weight_scale
        ).astype(jnp.bfloat16)
        image_part = jnp.dot(weights, partner_block, preferred_element_type=jnp.float32)
        text_part = across_rows(weights, image_bf)
        return (losses, image_part, text_part)

    own_loss, own_image, own_text = score_tile(text_bf, own_sign)
    near_loss, near_image, near_part = score_tile(near_text, -1.0)
    far_loss, far_image, far_part = score_tile(far_text, -1.0)
    diag_loss, diag_image, diag_part = score_tile(diag_text, -1.0)
    near_back = near_part.astype(jnp.bfloat16)
    far_back = far_part.astype(jnp.bfloat16)
    diag_back = diag_part.astype(jnp.bfloat16)

    def send_back(block, which_bit):
        return partner(block, ("wide", "narrow"), which_bit)

    from_near = send_back(near_back, near_bit)
    from_far = send_back(far_back, far_bit)
    from_diag = send_back(send_back(diag_back, far_bit), near_bit)
    local_loss = own_loss + near_loss + far_loss + diag_loss
    loss_total = lax.psum(local_loss, ("wide", "narrow"))
    loss = (loss_total / (block_rows * device_total)).reshape(1)
    image_dir = own_image + near_image + far_image + diag_image
    text_dir = (
        own_text
        + from_near.astype(jnp.float32)
        + from_far.astype(jnp.float32)
        + from_diag.astype(jnp.float32)
    )
    image_along = jnp.sum(image_unit * image_dir, axis=-1, keepdims=True)
    image_grad = ((image_dir - image_unit * image_along) / image_norm).astype(jnp.bfloat16)
    text_along = jnp.sum(text_unit * text_dir, axis=-1, keepdims=True)
    text_step = ((text_dir - text_unit * text_along) / text_norm).astype(jnp.bfloat16)
    text_grad = lax.dot_general(
        text_step, text_head, (((1,), (1,)), ((), ())), preferred_element_type=jnp.float32
    ).astype(jnp.bfloat16)
    group_feat = lax.all_to_all(text_feat, "narrow", split_axis=1, concat_axis=0, tiled=True)
    partial_rows = across_rows(group_feat, lax.all_gather(text_step, "narrow", axis=0, tiled=True))
    head_grad = lax.psum_scatter(partial_rows, "wide", scatter_dimension=1, tiled=True)
    return (image_grad, text_grad, head_grad, loss)


def solution(mesh):
    in_specs = (
        P(("wide", "narrow"), None),
        P(("wide", "narrow"), None),
        P(),
        P(("wide", "narrow")),
        P(("wide", "narrow")),
        P(),
        P(),
    )
    out_specs = (P(("wide", "narrow"), None), P(("wide", "narrow"), None), P("narrow", "wide"), P())
    return jax.shard_map(
        per_device, mesh=mesh, in_specs=in_specs, out_specs=out_specs, check_vma=False
    )
```

profile of v0, /device:TPU:1, one launch (start us, length us, event | category | flops | bytes accessed | tf_op | source)
XLA Modules:
  0.0 695.0 jit_solution(16093711860938709929)
XLA Ops:
  7.2 0.0 copy-start
  7.2 0.0 copy-start.2
  7.2 0.0 all-gather.2.cloned.1.call-start
  7.2 1.7 copy-done
  8.9 1.7 multiply_reduce_fusion.2
  10.6 0.8 fusion.19
  11.5 19.9 %collective-permute-start.1 = (bf16[128,1152]{1,0:T(8,128)(2,1)}, bf16[128,1152]{1,0:T(8,128)(2,1)}, u32[]{:S(2)}, u32[]{:S(2)}) collective-permute-start(bf16[128,1152]{1,0:T(8,128)(2,1)} %fusion.19), channel_id=1, source_target_pairs={{0,512},{1,513},{2,514},{3,515},{4,516},{5,517},{6,518},{7,519},{8... | collective-permute-start | bytes 884744 | tf_op jit(solution)/shard_map/ppermute | solution.py:10
  31.4 4.7 collective-permute-start
  38.0 0.1 fusion.5
  38.2 0.1 fusion.18
  38.3 1.8 fusion.4
  40.2 2.5 collective-permute-done
  42.6 1.9 collective-permute-start.2
  44.6 1.2 fusion.2
  45.8 0.0 collective-permute-done.1
  45.8 1.2 fusion.1
  47.0 40.5 %collective-permute-done.2 = bf16[128,1152]{1,0:T(8,128)(2,1)S(1)} collective-permute-done((bf16[128,1152]{1,0:T(8,128)(2,1)}, bf16[128,1152]{1,0:T(8,128)(2,1)S(1)}, u32[]{:S(2)}, u32[]{:S(2)}) %collective-permute-start.2) | collective-permute-done | bytes 294944 | tf_op jit(solution)/shard_map/ppermute | solution.py:10
  87.5 1.9 fusion.15
  89.5 0.3 convolution_convert_fusion.1
  89.8 3.2 collective-permute-start.5
  93.0 0.3 convolution_convert_fusion.2
  93.3 10.8 %collective-permute-start.4 = (bf16[128,1152]{1,0:T(8,128)(2,1)S(1)}, bf16[128,1152]{1,0:T(8,128)(2,1)S(1)}, u32[]{:S(2)}, u32[]{:S(2)}) collective-permute-start(bf16[128,1152]{1,0:T(8,128)(2,1)S(1)} %convolution_convert_fusion.2), channel_id=1, source_target_pairs={{0,512},{1,513},{2,514},{3,515},{4,516},{5,517},{6,518},{7,519},{8... | collective-permute-start | bytes 884744 | tf_op jit(solution)/shard_map/ppermute | solution.py:10
  104.2 0.3 convolution_convert_fusion.3
  104.5 5.8 collective-permute-start.3
  110.3 7.5 %collective-permute-done.5 = bf16[128,1152]{1,0:T(8,128)(2,1)S(1)} collective-permute-done((bf16[128,1152]{1,0:T(8,128)(2,1)S(1)}, bf16[128,1152]{1,0:T(8,128)(2,1)S(1)}, u32[]{:S(2)}, u32[]{:S(2)}) %collective-permute-start.5) | collective-permute-done | bytes 294944 | tf_op jit(solution)/shard_map/ppermute | solution.py:10
  117.8 10.9 %collective-permute-start.6 = (bf16[128,1152]{1,0:T(8,128)(2,1)S(1)}, bf16[128,1152]{1,0:T(8,128)(2,1)S(1)}, u32[]{:S(2)}, u32[]{:S(2)}) collective-permute-start(bf16[128,1152]{1,0:T(8,128)(2,1)S(1)} %collective-permute-done.5), channel_id=1, source_target_pairs={{0,8},{1,9},{2,10},{3,11},{4,12},{5,13},{6,14},{7,15},{8,0},{9,1},... | collective-permute-start | bytes 884744 | tf_op jit(solution)/shard_map/ppermute | solution.py:10
  128.8 6.7 collective-permute-done.6
  135.5 0.5 multiply_reduce_fusion
  136.1 0.9 divide_convert_fusion
  137.0 0.0 all-gather.2.cloned.1.call-update
  137.1 0.0 copy-start.4
  137.1 1.9 copy.15
  139.0 5.3 all-to-all-start
  144.3 0.0 all-reduce.3.cloned.1.call-start
  144.4 1.3 dynamic-slice
  146.3 1.3 fusion.17
  147.6 1.3 convolution_add_fusion.2
  148.9 1.3 convolution_add_fusion.1
  152.7 2.1 multiply_reduce_fusion.1
  154.9 113.3 %all-gather.2.cloned.1.call-done = bf16[2048,1152]{1,0:T(8,128)(2,1)} async-done(((bf16[128,1152]{1,0:T(8,128)(2,1)}), bf16[2048,1152]{1,0:T(8,128)(2,1)}) %all-gather.2.cloned.1.call-update) | async-done | bytes 4718608 | tf_op jit(solution)/shard_map/all_gather | solution.py:93
  268.2 4.0 convolution_bitcast_fusion
  272.1 0.0 all-reduce.3.cloned.1.call-update
  272.1 2.0 divide_convert_fusion.1
  274.1 125.5 %psum.7 = f32[]{:T(128)} all-reduce(f32[]{:T(128)S(6)} %add.113), channel_id=1, replica_groups=mesh['wide'=64,'narrow'=16] {'wide','narrow'}, use_global_device_ids=true, to_apply=%region_9.10 | all-reduce | flops 1 | bytes 8 | tf_op jit(solution)/shard_map/psum | solution.py:76
  400.3 1.6 convolution_convert_fusion
  401.9 283.5 %all-reduce.3.cloned.1.call-done = f32[72,1152]{1,0:T(8,128)} async-done(((f32[72,1152]{1,0:T(8,128)}), f32[72,1152]{1,0:T(8,128)}) %all-reduce.3.cloned.1.call-update) | async-done | bytes 331792
  685.4 1.0 constant_dynamic-slice_fusion
  686.4 0.7 copy.17
  (24 shorter events, 0.1 us)
Async XLA Ops:
  7.2 1.8 copy-start
  7.2 30.8 %copy-start.2 = (bf16[128,1152]{1,0:T(8,128)(2,1)S(1)}, bf16[128,1152]{1,0:T(8,128)(2,1)}, u32[]{:S(2)}) copy-start(bf16[128,1152]{1,0:T(8,128)(2,1)} %param.7) | copy-start | bytes 884740
  7.2 31.1 %copy-start.9 = (s32[128]{0:T(128)S(1)}, s32[128]{0:T(128)}, u32[]{:S(2)}) copy-start(s32[128]{0:T(128)} %param.11) | copy-start | bytes 1540
  7.2 261.0 %all-gather.2.cloned.1.call-start = ((), (), s32[]{:S(2)}) async-start(), calls=%async_computation.1 | async-start | bytes 5013504 | tf_op jit(solution)/shard_map/all_gather | solution.py:93
  8.9 29.3 %copy-start.3 = (bf16[128,1152]{1,0:T(8,128)(2,1)S(1)}, bf16[128,1152]{1,0:T(8,128)(2,1)}, u32[]{:S(2)}) copy-start(bf16[128,1152]{1,0:T(8,128)(2,1)} %param.7) | copy-start | bytes 884740
  11.5 34.3 %collective-permute-start.1 = (bf16[128,1152]{1,0:T(8,128)(2,1)}, bf16[128,1152]{1,0:T(8,128)(2,1)}, u32[]{:S(2)}, u32[]{:S(2)}) collective-permute-start(bf16[128,1152]{1,0:T(8,128)(2,1)} %fusion.19), channel_id=1, source_target_pairs={{0,512},{1,513},{2,514},{3,515},{4,516},{5,517},{6,518},{7,519},{8... | collective-permute-start | bytes 884744 | tf_op jit(solution)/shard_map/ppermute | solution.py:10
  31.4 11.3 %collective-permute-start = (bf16[128,1152]{1,0:T(8,128)(2,1)}, bf16[128,1152]{1,0:T(8,128)(2,1)}, u32[]{:S(2)}, u32[]{:S(2)}) collective-permute-start(bf16[128,1152]{1,0:T(8,128)(2,1)} %fusion.19), channel_id=1, source_target_pairs={{0,8},{1,9},{2,10},{3,11},{4,12},{5,13},{6,14},{7,15},{8,0},{9,1},... | collective-permute-start | bytes 884744 | tf_op jit(solution)/shard_map/ppermute | solution.py:10
  40.2 95.3 %copy-start.7 = (f32[128,128]{1,0:T(8,128)S(1)}, f32[128,128]{1,0:T(8,128)}, u32[]{:S(2)}) copy-start(f32[128,128]{1,0:T(8,128)} %fusion.4) | copy-start | bytes 196612
  42.6 44.9 %collective-permute-start.2 = (bf16[128,1152]{1,0:T(8,128)(2,1)}, bf16[128,1152]{1,0:T(8,128)(2,1)S(1)}, u32[]{:S(2)}, u32[]{:S(2)}) collective-permute-start(bf16[128,1152]{1,0:T(8,128)(2,1)} %collective-permute-done), channel_id=1, source_target_pairs={{0,512},{1,513},{2,514},{3,515},{4,516},{5,517},{6,518},{7,519},{8... | collective-permute-start | bytes 884744 | tf_op jit(solution)/shard_map/ppermute | solution.py:10
  45.8 90.3 %copy-start.5 = (f32[128,128]{1,0:T(8,128)}, f32[128,128]{1,0:T(8,128)S(1)}, u32[]{:S(2)}) copy-start(f32[128,128]{1,0:T(8,128)S(1)} %fusion.2) | copy-start | bytes 196612
  47.0 89.0 %copy-start.6 = (f32[128,128]{1,0:T(8,128)}, f32[128,128]{1,0:T(8,128)S(1)}, u32[]{:S(2)}) copy-start(f32[128,128]{1,0:T(8,128)S(1)} %fusion.1) | copy-start | bytes 196612
  87.5 48.5 %copy-start.10 = (bf16[128,1152]{1,0:T(8,128)(2,1)}, bf16[128,1152]{1,0:T(8,128)(2,1)S(1)}, u32[]{:S(2)}) copy-start(bf16[128,1152]{1,0:T(8,128)(2,1)S(1)} %collective-permute-done.2) | copy-start | bytes 884740
  89.5 46.6 %copy-start.8 = (f32[128,128]{1,0:T(8,128)}, f32[128,128]{1,0:T(8,128)S(1)}, u32[]{:S(2)}) copy-start(f32[128,128]{1,0:T(8,128)S(1)} %get-tuple-element.26) | copy-start | bytes 196612
  89.8 28.0 %collective-permute-start.5 = (bf16[128,1152]{1,0:T(8,128)(2,1)S(1)}, bf16[128,1152]{1,0:T(8,128)(2,1)S(1)}, u32[]{:S(2)}, u32[]{:S(2)}) collective-permute-start(bf16[128,1152]{1,0:T(8,128)(2,1)S(1)} %convolution_convert_fusion.1), channel_id=1, source_target_pairs={{0,512},{1,513},{2,514},{3,515},{4,516},{5,517},{6,518},{7,519},{8... | collective-permute-start | bytes 884744 | tf_op jit(solution)/shard_map/ppermute | solution.py:10
  93.3 35.4 %collective-permute-start.4 = (bf16[128,1152]{1,0:T(8,128)(2,1)S(1)}, bf16[128,1152]{1,0:T(8,128)(2,1)S(1)}, u32[]{:S(2)}, u32[]{:S(2)}) collective-permute-start(bf16[128,1152]{1,0:T(8,128)(2,1)S(1)} %convolution_convert_fusion.2), channel_id=1, source_target_pairs={{0,512},{1,513},{2,514},{3,515},{4,516},{5,517},{6,518},{7,519},{8... | collective-permute-start | bytes 884744 | tf_op jit(solution)/shard_map/ppermute | solution.py:10
  104.5 24.3 %collective-permute-start.3 = (bf16[128,1152]{1,0:T(8,128)(2,1)S(1)}, bf16[128,1152]{1,0:T(8,128)(2,1)S(1)}, u32[]{:S(2)}, u32[]{:S(2)}) collective-permute-start(bf16[128,1152]{1,0:T(8,128)(2,1)S(1)} %convolution_convert_fusion.3), channel_id=1, source_target_pairs={{0,8},{1,9},{2,10},{3,11},{4,12},{5,13},{6,14},{7,15},{8,0},{9,1},... | collective-permute-start | bytes 884744 | tf_op jit(solution)/shard_map/ppermute | solution.py:10
  117.8 17.7 %collective-permute-start.6 = (bf16[128,1152]{1,0:T(8,128)(2,1)S(1)}, bf16[128,1152]{1,0:T(8,128)(2,1)S(1)}, u32[]{:S(2)}, u32[]{:S(2)}) collective-permute-start(bf16[128,1152]{1,0:T(8,128)(2,1)S(1)} %collective-permute-done.5), channel_id=1, source_target_pairs={{0,8},{1,9},{2,10},{3,11},{4,12},{5,13},{6,14},{7,15},{8,0},{9,1},... | collective-permute-start | bytes 884744 | tf_op jit(solution)/shard_map/ppermute | solution.py:10
  137.1 15.7 %copy-start.4 = (bf16[128,1152]{1,0:T(8,128)(2,1)S(1)}, bf16[128,1152]{1,0:T(8,128)(2,1)}, u32[]{:S(2)}) copy-start(bf16[128,1152]{1,0:T(8,128)(2,1)} %param.7) | copy-start | bytes 884740
  139.0 15.9 %all-to-all-start = ((bf16[128,16,72]{0,2,1:T(8,128)(2,1)}), bf16[128,16,72]{0,2,1:T(8,128)(2,1)}, u32[]{:S(2)}, u32[]{:S(2)}) async-start(bf16[128,16,72]{0,2,1:T(8,128)(2,1)} %bitcast.3), calls=%async_computation | async-start | bytes 589824 | tf_op jit(solution)/shard_map/all_to_all | solution.py:92
  144.3 541.1 %all-reduce.3.cloned.1.call-start = ((), (), s32[]{:S(2)}) async-start(), calls=%async_computation.2 | async-start | bytes 663552
  154.9 245.4 %copy-start.1 = (bf16[128,1152]{1,0:T(8,128)(2,1)S(1)}, bf16[128,1152]{1,0:T(8,128)(2,1)}, u32[]{:S(2)}) copy-start(bf16[128,1152]{1,0:T(8,128)(2,1)} %divide_convert_fusion) | copy-start | bytes 884740
Sparse Core Ops, SparseCore 0:
  137.2 130.9 all-gather.1
  272.3 413.0 all-reduce.2
where the time goes:
time: 698 us; the launch traced here: 695 us
  waiting for transfers between devices  454 us (65%)
  blocking collectives  126 us (18%)
  starting transfers between devices  62.6 us (9%)
  between operations  21.3 us (3%)
  matrix products  21 us (3%)
    unnamed x3, waiting for transfers between devices  284 us
    psum x1, blocking collectives, per_device(): loss_total = lax.psum(local_loss, ('wide', 'narrow'))  126 us
    all_gather x1, waiting for transfers between devices, per_device(): lax.all_gather(text_step, 'narrow', axis=0, tiled=True)  113 us
    ppermute x7, waiting for transfers between devices, partner(): lax.ppermute(value, axis, [(i, i ^ 1 << stride) for i in range(lax.axis_s...  57.2 us
    ppermute x7, starting transfers between devices, partner(): lax.ppermute(value, axis, [(i, i ^ 1 << stride) for i in range(lax.axis_s...  57.1 us
  transfers between devices with their start and end apart: 10, of which 6 were waited for; matrix products, arithmetic and copies ran while one was open for 3% of the time, Pallas kernels for 0%

commit v1 on v0

v1 whole, which is shorter than its diff:
```python
import jax
import jax.numpy as jnp
from jax import lax
from jax.experimental import pallas as pl
from jax.experimental.pallas import tpu as pltpu
from jax.sharding import PartitionSpec as P

EPSILON = 1e-06
VMEM_BYTES = int(53.2 * 2**20)
MESH = pl.DeviceIdType.MESH
F32 = jnp.float32
BF16 = jnp.bfloat16

ROWS = 128
WIDTH = 1152
N_Z = 16
N_Y = 8
N_X = 4
DEVICES = 1024
CHUNKS = 4
CHUNK = ROWS // CHUNKS
HALF = WIDTH // 2
QUARTER = WIDTH // 4
OUT_ROWS = WIDTH // 16
OUT_COLS = WIDTH // 64
Y_PAD = 80
Z_PAD = 32
STEP_ROWS = QUARTER + 16

X_PEERS = [(dx, dc) for dx in (2, 1, 3, 0) for dc in range(2) if (dx, dc) != (0, 0)]


def position():
    wide, narrow = lax.axis_index("wide"), lax.axis_index("narrow")
    return {
        "z": wide // 4,
        "x": (narrow // N_Y) * 2 + (wide // 2) % 2,
        "core": wide % 2,
        "y": narrow % N_Y,
    }


def moved(pos, dz=0, dy=0, dx=0, dc=0):
    return {
        "z": (pos["z"] + dz) % N_Z,
        "y": (pos["y"] + dy) % N_Y,
        "x": (pos["x"] + dx) % N_X,
        "core": (pos["core"] + dc) % 2,
    }


def flipped(pos, bit):
    return dict(pos, z=pos["z"] + bit - 2 * bit * ((pos["z"] // bit) % 2))


def device_of(pos):
    return (
        pos["z"] * 4 + (pos["x"] % 2) * 2 + pos["core"],
        (pos["x"] // 2) * N_Y + pos["y"],
    )


def nt(left, right):
    return lax.dot_general(left, right, (((1,), (1,)), ((), ())), preferred_element_type=F32)


def tn(left, right):
    return lax.dot_general(left, right, (((0,), (0,)), ((), ())), preferred_element_type=F32)


def thirds(value):
    high = value.astype(BF16).astype(F32)
    middle = (value - high).astype(BF16).astype(F32)
    low = value - high - middle
    row = lax.broadcasted_iota(jnp.int32, (8, ROWS), 0)
    return jnp.where(row == 0, high, jnp.where(row == 1, middle, jnp.where(row == 2, low, 0.0)))


def whole(rows):
    return jnp.sum(rows, axis=0, keepdims=True)


def nn(left, right):
    return jnp.dot(left, right, preferred_element_type=F32)


def kernel(
    image_in, feat_in, head_in, positive_in, counts_ref, log_scale_ref, bias_ref,
    image_grad_ref, text_grad_ref, head_grad_ref, loss_ref,
    image_ref, feat_ref, head_ref, positive_ref,
    image_own, text_own, image_near, text_near, image_far, text_far, image_diag, text_diag,
    text_unit, text_dir, image_dir, feat_t, feat_all, step_t, step_q, step_out, step_all,
    head_part, y_send, y_recv, z_part, z_send, z_recv,
    send_sem, recv_sem, local_sem, round_sem,
):
    loads = [
        pltpu.make_async_copy(source, target, local_sem.at[2 + i])
        for i, (source, target) in enumerate(
            [
                (image_in, image_ref),
                (feat_in, feat_ref),
                (head_in, head_ref),
                (positive_in, positive_ref),
            ]
        )
    ]
    for load in loads:
        load.start()
    pos = position()
    peers = {"far": moved(pos, dz=8), "near": moved(pos, dx=2)}
    barrier = pltpu.get_barrier_semaphore()
    greeted = (
        [flipped(pos, bit) for bit in (8, 4, 2, 1)]
        + [moved(pos, dy=dy) for dy in range(1, N_Y)]
        + [moved(pos, dx=dx, dc=dc) for dx, dc in X_PEERS]
    )
    for peer in greeted:
        pl.semaphore_signal(barrier, inc=1, device_id=device_of(peer), device_id_type=MESH)

    used = []

    def send(source, target, peer):
        slot = len(used)
        copy = pltpu.make_async_remote_copy(
            src_ref=source,
            dst_ref=target,
            send_sem=send_sem.at[slot],
            recv_sem=recv_sem.at[slot],
            device_id=device_of(peer),
            device_id_type=MESH,
        )
        copy.start()
        used.append(copy)
        return copy

    def tell(bit):
        pl.semaphore_signal(
            round_sem.at[bit // 2], inc=1, device_id=device_of(flipped(pos, bit)), device_id_type=MESH
        )

    def told(bit):
        pl.semaphore_wait(round_sem.at[bit // 2], 1)

    def arrived(copies):
        for copy in copies:
            copy.wait_recv()

    scale = jnp.exp(jnp.full((1, 1), log_scale_ref[0], F32))
    bias = jnp.full((1, 1), bias_ref[0], F32)
    weight_scale = scale / ROWS
    count = counts_ref[0]
    live_rows = lax.broadcasted_iota(jnp.int32, (ROWS, 1), 0) < count
    live_lanes = (lax.broadcasted_iota(jnp.int32, (1, ROWS), 1) < count).astype(F32)

    def image_rows():
        rows = image_ref[...].astype(F32)
        norm = jnp.sqrt(jnp.sum(rows * rows, axis=-1, keepdims=True) + EPSILON)
        return rows / norm, norm

    loads[0].wait()
    image_own[...] = jnp.where(live_rows, image_rows()[0], 0.0).astype(BF16)

    pl.semaphore_wait(barrier, len(greeted))

    def chunk(ref, index):
        return ref.at[pl.ds(index * CHUNK, CHUNK)]

    image_out = [send(chunk(image_own, i), chunk(image_far, i), peers["far"]) for i in range(CHUNKS)]
    image_near_copy = send(image_own, image_near, peers["near"])

    tell(1)

    loads[1].wait()
    feat_t[...] = jnp.transpose(feat_ref[...].astype(F32)).astype(BF16)
    own_lanes = pl.ds(pl.multiple_of((pos["x"] * 2 + pos["core"]) * ROWS, ROWS), ROWS)

    def feat_rows(peer):
        return feat_t.at[pl.ds(pl.multiple_of((peer["x"] // 2) * HALF, HALF), HALF)]

    feat_copies = []
    for dx, dc in X_PEERS:
        peer = moved(pos, dx=dx, dc=dc)
        feat_copies.append(send(feat_rows(peer), feat_all.at[:, own_lanes], peer))
    own_feat = pltpu.make_async_copy(feat_rows(pos), feat_all.at[:, own_lanes], local_sem.at[0])
    own_feat.start()

    y_send[...] = jnp.zeros(y_send.shape, BF16)
    z_part[...] = jnp.zeros(z_part.shape, F32)
    loads[2].wait()
    projected = nn(feat_ref[...], head_ref[...])
    text_norm = jnp.sqrt(jnp.sum(projected * projected, axis=-1, keepdims=True) + EPSILON)
    text_unit[...] = projected / text_norm
    text_own[...] = text_unit[...].astype(BF16)
    text_near_copy = send(text_own, text_near, peers["near"])

    def tile(text, image, sign):
        logits = scale * nt(text, image) + bias
        turned = -sign * logits
        decay = jnp.exp(-jnp.abs(turned))
        losses = jnp.maximum(turned, 0.0) + jnp.log1p(decay)
        weights = -sign * (jnp.where(turned >= 0, 1.0, decay) / (1.0 + decay)) * weight_scale
        return losses, weights

    def total(values):
        return jnp.sum(jnp.sum(values, axis=0, keepdims=True), axis=1, keepdims=True)

    loads[3].wait()
    matches = lax.broadcasted_iota(jnp.int32, (ROWS, ROWS), 0) == positive_ref[...]
    losses, weights = tile(text_own[...], image_own[...], jnp.where(matches, 1.0, -1.0).astype(F32))
    local_loss = total(losses * live_lanes)
    weights = (weights * live_lanes).astype(BF16)
    text_dir[...] = nn(weights, image_own[...])
    image_dir[...] = tn(weights, text_own[...])

    def text_side(image):
        losses, weights = tile(text_own[...], image[...], -1.0)
        text_dir[...] += nn(weights.astype(BF16), image[...])
        return total(losses)

    def image_side(text):
        _, weights = tile(text[...], image_own[...], -1.0)
        image_dir[...] += tn((weights * live_lanes).astype(BF16), text[...])

    arrived([image_near_copy])
    local_loss += text_side(image_near)
    arrived([text_near_copy])
    image_side(text_near)

    image_diag_copies, text_out = [], []
    for i in range(CHUNKS):
        arrived([image_out[i]])
        image_diag_copies.append(send(chunk(image_far, i), chunk(image_diag, i), peers["near"]))
        text_out.append(send(chunk(text_own, i), chunk(text_far, i), peers["far"]))
    local_loss += text_side(image_far)
    arrived(image_diag_copies)
    local_loss += text_side(image_diag)
    dead_loss = jnp.maximum(bias, 0.0) + jnp.log1p(jnp.exp(-jnp.abs(bias)))
    dead_pairs = (3 * ROWS * (ROWS - jnp.full((1, 1), count, jnp.int32))).astype(F32)
    local_loss -= dead_loss * dead_pairs

    direction = text_dir[...]
    along = jnp.sum(text_unit[...] * direction, axis=-1, keepdims=True)
    step = ((direction - text_unit[...] * along) / text_norm).astype(BF16)
    step_t[...] = jnp.transpose(step.astype(F32))
    for quarter in range(4):
        for z in range(N_Z):
            step_q[quarter * QUARTER + z * OUT_COLS : quarter * QUARTER + (z + 1) * OUT_COLS, :] = step_t[
                (z * 4 + quarter) * OUT_COLS : (z * 4 + quarter + 1) * OUT_COLS, :
            ]
    loss_rows = jnp.concatenate([thirds(local_loss), jnp.zeros((STEP_ROWS - QUARTER - 8, ROWS), F32)], axis=0)
    for quarter in range(4):
        start = quarter * STEP_ROWS
        step_out[start : start + QUARTER, :] = step_q[quarter * QUARTER : (quarter + 1) * QUARTER, :].astype(BF16)
        step_out[start + QUARTER : start + STEP_ROWS, :] = loss_rows.astype(BF16)

    def step_rows(peer):
        quarter = (peer["x"] % 2) * 2 + peer["core"]
        return step_out.at[pl.ds(pl.multiple_of(quarter * STEP_ROWS, STEP_ROWS), STEP_ROWS)]

    step_copies = []
    for dx, dc in X_PEERS:
        peer = moved(pos, dx=dx, dc=dc)
        step_copies.append(send(step_rows(peer), step_all.at[:, own_lanes], peer))
    own_step = pltpu.make_async_copy(step_rows(pos), step_all.at[:, own_lanes], local_sem.at[1])
    own_step.start()

    text_grad_ref[...] = nt(step, head_ref[...]).astype(BF16)
    told(1)
    tell(2)

    arrived(feat_copies)
    own_feat.wait()
    arrived(step_copies)
    own_step.wait()
    head_part[...] = nt(feat_all[...], step_all[0:QUARTER, :])
    parts = step_all[QUARTER:STEP_ROWS, :].astype(F32)
    line_loss = thirds(sum(whole(parts[:, i * ROWS : (i + 1) * ROWS]) for i in range(8))[:, 0:1])
    y_copies = []
    for slot, dy in enumerate(sorted(range(1, N_Y), key=lambda d: -min(d, N_Y - d))):
        peer = moved(pos, dy=dy)
        rows = head_part[pl.ds(pl.multiple_of(peer["y"] * OUT_ROWS, OUT_ROWS), OUT_ROWS), :]
        y_send[slot, 0:OUT_ROWS, :] = rows.astype(BF16)
        y_send[slot, OUT_ROWS:Y_PAD, 0:ROWS] = line_loss.astype(BF16)
        y_copies.append(send(y_send.at[slot], y_recv.at[slot], peer))
    told(2)
    tell(4)
    text_diag_copies = []
    for i in range(CHUNKS):
        arrived([text_out[i]])
        text_diag_copies.append(send(chunk(text_far, i), chunk(text_diag, i), peers["near"]))

    arrived(y_copies)
    rows = head_part[pl.ds(pl.multiple_of(pos["y"] * OUT_ROWS, OUT_ROWS), OUT_ROWS), :]
    for index in range(N_Y - 1):
        rows += y_recv[index, 0:OUT_ROWS, :].astype(F32)
        line_loss += y_recv[index, OUT_ROWS:Y_PAD, 0:ROWS].astype(F32)
    plane_loss = thirds(whole(line_loss)[:, 0:1])
    rows = jnp.concatenate([rows, jnp.zeros((OUT_ROWS, 3 * ROWS - QUARTER), F32)], axis=1)
    rows = jnp.concatenate([rows, jnp.zeros((ROWS - OUT_ROWS, 3 * ROWS), F32)], axis=0)
    step_t[0 : 3 * ROWS, :] = jnp.transpose(rows)
    for z in range(N_Z):
        z_part[z, 0:OUT_COLS, :] = step_t[z * OUT_COLS : (z + 1) * OUT_COLS, :]
        z_part[z, OUT_COLS : OUT_COLS + 3, :] = plane_loss[0:3, :]
    z_send[...] = z_part[...].astype(BF16)

    told(4)
    z_copies = []
    for dz in sorted(range(1, N_Z), key=lambda d: -min(d, N_Z - d)):
        peer = moved(pos, dz=dz)
        z_copies.append(send(z_send.at[peer["z"]], z_recv.at[dz - 1], peer))

    image_side(text_far)
    arrived(text_diag_copies)
    image_side(text_diag)
    unit, norm = image_rows()
    direction = image_dir[...]
    along = jnp.sum(unit * direction, axis=-1, keepdims=True)
    image_grad_ref[...] = ((direction - unit * along) / norm).astype(BF16)

    arrived(z_copies)
    block = z_part[pos["z"]]
    for index in range(N_Z - 1):
        block += z_recv[index].astype(F32)
    head_grad_ref[...] = block[0:OUT_COLS, 0:OUT_ROWS]
    loss_ref[...] = whole(block[OUT_COLS : OUT_COLS + 3, 0:1]) / (ROWS * DEVICES)
    for copy in used:
        copy.wait_send()


COPIES = 2 * CHUNKS * 2 + 2 + 2 * len(X_PEERS) + (N_Y - 1) + (N_Z - 1)


def per_device(image_emb, text_feat, text_head, row_counts, positive, log_scale, logit_bias):
    vmem = pl.BlockSpec(memory_space=pltpu.VMEM)
    smem = pl.BlockSpec(memory_space=pltpu.SMEM)
    hbm = pl.BlockSpec(memory_space=pltpu.HBM)
    block = pltpu.VMEM((ROWS, WIDTH), BF16)
    wide_block = pltpu.VMEM((ROWS, WIDTH), F32)
    image_grad, text_grad, head_grad, loss = pl.pallas_call(
        kernel,
        name="sigmoid_loss_step",
        out_shape=(
            jax.ShapeDtypeStruct((ROWS, WIDTH), BF16),
            jax.ShapeDtypeStruct((ROWS, WIDTH), BF16),
            jax.ShapeDtypeStruct((OUT_COLS, OUT_ROWS), F32),
            jax.ShapeDtypeStruct((1, 1), F32),
        ),
        in_specs=[hbm, hbm, hbm, hbm, smem, smem, smem],
        out_specs=(vmem, vmem, vmem, vmem),
        scratch_shapes=[block, block, pltpu.VMEM((WIDTH, WIDTH), BF16), pltpu.VMEM((1, ROWS), jnp.int32)]
        + [block] * 8
        + [wide_block] * 3
        + [
            pltpu.VMEM((WIDTH, ROWS), BF16),
            pltpu.VMEM((HALF, 8 * ROWS), BF16),
            pltpu.VMEM((WIDTH, ROWS), F32),
            pltpu.VMEM((WIDTH, ROWS), F32),
            pltpu.VMEM((4 * STEP_ROWS, ROWS), BF16),
            pltpu.VMEM((STEP_ROWS, 8 * ROWS), BF16),
            pltpu.VMEM((HALF, QUARTER), F32),
            pltpu.VMEM((N_Y - 1, Y_PAD, QUARTER), BF16),
            pltpu.VMEM((N_Y - 1, Y_PAD, QUARTER), BF16),
            pltpu.VMEM((N_Z, Z_PAD, ROWS), F32),
            pltpu.VMEM((N_Z, Z_PAD, ROWS), BF16),
            pltpu.VMEM((N_Z - 1, Z_PAD, ROWS), BF16),
            pltpu.SemaphoreType.DMA((COPIES,)),
            pltpu.SemaphoreType.DMA((COPIES,)),
            pltpu.SemaphoreType.DMA((6,)),
            pltpu.SemaphoreType.REGULAR((3,)),
        ],
        compiler_params=pltpu.CompilerParams(
            collective_id=0, has_side_effects=True, vmem_limit_bytes=VMEM_BYTES
        ),
    )(image_emb, text_feat, text_head, positive.reshape(1, ROWS), row_counts, log_scale, logit_bias)
    return image_grad, text_grad, head_grad.T, loss.reshape(1)


def solution(mesh):
    rows = P(("wide", "narrow"), None)
    blocks = P(("wide", "narrow"))
    return jax.shard_map(
        per_device,
        mesh=mesh,
        in_specs=(rows, rows, P(), blocks, blocks, P(), P()),
        out_specs=(rows, rows, P("narrow", "wide"), P()),
        check_vma=False,
    )
```

time: 698 us -> 99.4 us (0.14)
  waiting for transfers between devices: 454 us -> 0 us
  blocking collectives: 126 us -> 0 us
  Pallas kernels: 0 us -> 92.2 us
  starting transfers between devices: 62.6 us -> 0 us
  matrix products: 21 us -> 0 us
  between operations: 21.3 us -> 4.35 us
    unnamed x3 -> x0, waiting for transfers between devices: 284 us -> none
    psum x1 -> x0, blocking collectives: 126 us -> none  [per_device(): loss_total = lax.psum(local_loss, ('wide', 'narrow'))]
    all_gather x1 -> x0, waiting for transfers between devices: 113 us -> none  [per_device(): lax.all_gather(text_step, 'narrow', axis=0, tiled=True)]
    pallas_call x0 -> x1, Pallas kernels: none -> 92.2 us  [per_device(): pl.pallas_call(kernel, name='sigmoid_loss_step', out_shape=(jax.ShapeDtyp...]
    ppermute x7 -> x0, waiting for transfers between devices: 57.2 us -> none  [partner(): lax.ppermute(value, axis, [(i, i ^ 1 << stride) for i in range(lax.axis_s...]
    ppermute x7 -> x0, starting transfers between devices: 57.1 us -> none  [partner(): lax.ppermute(value, axis, [(i, i ^ 1 << stride) for i in range(lax.axis_s...]
    dot_general x15 -> x0, matrix products: 21 us -> none  [the longest x4 6.2 us: score_tile(): lax.dot_general(image_bf, partner_block, (((1,), (1,)), ((), ())), prefer...]
  transfers between devices with their start and end apart: 10 -> 0, of which waited for: 6 -> 0; matrix products, arithmetic and copies ran while one was open for 3% -> 0% of each run, Pallas kernels for 0% -> 0%
where the time goes in v1:
time: 99.4 us; the launch traced here: 99.2 us
  Pallas kernels  92.2 us (93%)
  between operations  4.35 us (4%)
  local copies, waits for them, and re-layouts  2.68 us (3%)
    pallas_call x1, Pallas kernels, per_device(): pl.pallas_call(kernel, name='sigmoid_loss_step', out_shape=(jax.ShapeDtyp...  92.2 us
    unnamed x5, local copies, waits for them, and re-layouts  2.68 us

profile of v1, /device:TPU:1, one launch (start us, length us, event | category | flops | bytes accessed | tf_op | source)
XLA Modules:
  0.0 99.2 jit_solution(15037776057282363585)
XLA Ops:
  2.6 0.0 copy-start
  2.6 0.6 copy-done
  3.2 92.2 %sigmoid_loss_step.1 = (bf16[128,1152]{1,0:T(8,128)(2,1)S(1)}, bf16[128,1152]{1,0:T(8,128)(2,1)S(1)}, f32[18,72]{1,0:T(8,128)S(1)}, f32[1,1]{1,0:T(1,128)}) custom-call(bf16[128,1152]{1,0:T(8,128)(2,1)} %image_in.1, bf16[128,1152]{1,0:T(8,128)(2,1)} %feat_in.1, bf16[1152,1152]{1,0:T(8,128)(2,1)} %head_in.1, s32[1,128]{1,0:T(1,128)S(1)} %bitcast.4, ...), custom_call_target="tpu_custom_call" | custom-call | tf_op jit(solution)/shard_map/sigmoid_loss_step/pallas_call | solution.py:339
  95.4 0.7 copy.18
  96.1 0.7 copy.19
  96.8 0.6 copy.20
Async XLA Ops:
  2.6 0.7 copy-start

commit v2 on v1

--- a/solution.py
+++ b/solution.py
@@ -24,7 +24,7 @@
 OUT_ROWS = WIDTH // 16
 OUT_COLS = WIDTH // 64
 Y_PAD = 80
-Z_PAD = 32
+Z_PAD = 16
 STEP_ROWS = QUARTER + 16
 
 X_PEERS = [(dx, dc) for dx in (2, 1, 3, 0) for dc in range(2) if (dx, dc) != (0, 0)]
@@ -185,7 +185,6 @@
     own_feat.start()
 
     y_send[...] = jnp.zeros(y_send.shape, BF16)
-    z_part[...] = jnp.zeros(z_part.shape, F32)
     loads[2].wait()
     projected = nn(feat_ref[...], head_ref[...])
     text_norm = jnp.sqrt(jnp.sum(projected * projected, axis=-1, keepdims=True) + EPSILON)
@@ -298,9 +297,17 @@
     rows = jnp.concatenate([rows, jnp.zeros((OUT_ROWS, 3 * ROWS - QUARTER), F32)], axis=1)
     rows = jnp.concatenate([rows, jnp.zeros((ROWS - OUT_ROWS, 3 * ROWS), F32)], axis=0)
     step_t[0 : 3 * ROWS, :] = jnp.transpose(rows)
+    lane = lax.broadcasted_iota(jnp.int32, (8, ROWS), 1)
+    row = lax.broadcasted_iota(jnp.int32, (8, ROWS), 0)
+    loss_rows = pltpu.roll(plane_loss, 4, 0)
     for z in range(N_Z):
-        z_part[z, 0:OUT_COLS, :] = step_t[z * OUT_COLS : (z + 1) * OUT_COLS, :]
-        z_part[z, OUT_COLS : OUT_COLS + 3, :] = plane_loss[0:3, :]
+        start = z * OUT_COLS
+        last = step_t[start + 16 : start + 24, :]
+        front = pltpu.roll(last, OUT_ROWS, 1)
+        back = pltpu.roll(pltpu.roll(last, OUT_ROWS // 2, 1), 2, 0)
+        spare = jnp.where(row < 2, front, jnp.where(row < 4, back, loss_rows))
+        z_part[z, 0:8, :] = jnp.where(lane < OUT_ROWS, step_t[start : start + 8, :], spare)
+        z_part[z, 8:16, :] = step_t[start + 8 : start + 16, :]
     z_send[...] = z_part[...].astype(BF16)
 
     told(4)
@@ -321,8 +328,13 @@
     block = z_part[pos["z"]]
     for index in range(N_Z - 1):
         block += z_recv[index].astype(F32)
-    head_grad_ref[...] = block[0:OUT_COLS, 0:OUT_ROWS]
-    loss_ref[...] = whole(block[OUT_COLS : OUT_COLS + 3, 0:1]) / (ROWS * DEVICES)
+    first = block[0:8, :]
+    front = pltpu.roll(first, ROWS - OUT_ROWS, 1)
+    back = pltpu.roll(pltpu.roll(first, ROWS - OUT_ROWS // 2, 1), 6, 0)
+    last = jnp.where(lane < OUT_ROWS // 2, front, back)
+    head_grad_ref[0:16, :] = block[:, 0:OUT_ROWS]
+    head_grad_ref[16:OUT_COLS, :] = last[0 : OUT_COLS - 16, 0:OUT_ROWS]
+    loss_ref[...] = whole(first[4:7, ROWS - 1 : ROWS]) / (ROWS * DEVICES)
     for copy in used:
         copy.wait_send()
 

time: 99.4 us -> 97.3 us (0.979)
  Pallas kernels: 92.2 us -> 90 us
    pallas_call x1, Pallas kernels: 92.2 us -> 90 us  [per_device(): pl.pallas_call(kernel, name='sigmoid_loss_step', out_shape=(jax.ShapeDtyp...]
where the time goes in v2:
time: 97.3 us; the launch traced here: 97.1 us
  Pallas kernels  90 us (92%)
  between operations  4.35 us (4%)
  local copies, waits for them, and re-layouts  2.68 us (3%)
    pallas_call x1, Pallas kernels, per_device(): pl.pallas_call(kernel, name='sigmoid_loss_step', out_shape=(jax.ShapeDtyp...  90 us
    unnamed x5, local copies, waits for them, and re-layouts  2.68 us

profile of v2, /device:TPU:1, one launch (start us, length us, event | category | flops | bytes accessed | tf_op | source)
XLA Modules:
  0.0 97.1 jit_solution(15705985708941023568)
XLA Ops:
  2.6 0.0 copy-start
  2.6 0.6 copy-done
  3.2 90.0 %sigmoid_loss_step.1 = (bf16[128,1152]{1,0:T(8,128)(2,1)S(1)}, bf16[128,1152]{1,0:T(8,128)(2,1)S(1)}, f32[18,72]{1,0:T(8,128)S(1)}, f32[1,1]{1,0:T(1,128)}) custom-call(bf16[128,1152]{1,0:T(8,128)(2,1)} %image_in.1, bf16[128,1152]{1,0:T(8,128)(2,1)} %feat_in.1, bf16[1152,1152]{1,0:T(8,128)(2,1)} %head_in.1, s32[1,128]{1,0:T(1,128)S(1)} %bitcast.4, ...), custom_call_target="tpu_custom_call" | custom-call | tf_op jit(solution)/shard_map/sigmoid_loss_step/pallas_call | solution.py:351
  93.3 0.7 copy.18
  94.0 0.7 copy.19
  94.7 0.6 copy.20
Async XLA Ops:
  2.6 0.7 copy-start
